TPU v7x, 256 devices: a whole 4x4x8 slice. The times are simulated.
256 devices in a mesh: row: 64 (over z, y, core), col: 4 (over x).
Axes of the slice: x: 4, y: 4, z: 8, core: 2. Of those that a mesh axis runs over, the one named last changes fastest.
Arguments:
- density_panel: bfloat16 [32768, 256], P('row'), may hold values from -6 to 6
- blocks: bfloat16 [98304, 4096], P(('row', 'col')), may hold values from -0.0625 to 0.0625
- block_row: int32 [98304], P(('row', 'col')), may hold values from 0 to 7
- block_slot: int32 [98304], P(('row', 'col')), may hold values from -1 to 127, as said below
- requests: int32 [16384, 2], P(('row', 'col')), may hold values from -1 to 7, as said below
Outputs:
- first_product: bfloat16 [32768, 256], P('row')
- second_product: bfloat16 [32768, 256], P('row')
Inputs may be any that keep to these rules, and one draw needn't show every extreme that they name: requests[d * 64 + o, t] is -1 or t * 4 + d % 4; it is -1 whenever o < d // 4 and never when o = d // 4. A live block's slot holds a request other than -1, bi <= bj, and no two live blocks of one list share both block_row and block_slot.
All inputs are finite; a program needn't handle non-finite values.
Results may differ from a plain program's by a relative error of at most 0.0039.
Values may be sent and summed in bfloat16 or wider, within the bound.
A program may use at most 128 MiB of HBM per device.

v0:
```python
import jax
import jax.numpy as jnp
from jax import lax
from jax.sharding import PartitionSpec as P

B = 64
K = 256
GROUP_BLOCK_ROWS = 8


def build_matrix(blocks, block_row, block_slot, slot_count):
    stored = blocks.shape[0]
    pieces = blocks.reshape(stored, B, B)
    target = jnp.where(block_slot >= 0, block_slot, slot_count)
    zero_blocks = jnp.zeros((GROUP_BLOCK_ROWS, slot_count, B, B), blocks.dtype)
    return zero_blocks.at[block_row, target].set(pieces, mode="drop")


def serve_rows(local_rows, wanted):
    row_blocks = local_rows.reshape(GROUP_BLOCK_ROWS, B, K)
    picked = jnp.take(row_blocks, jnp.maximum(wanted, 0), axis=0)
    present = (wanted >= 0)[:, :, None, None]
    return jnp.where(present, picked, jnp.zeros_like(picked))


def request_rows(local_rows, requests):
    wanted = lax.all_to_all(requests, "row", split_axis=0, concat_axis=0, tiled=True)
    answer_rows = lax.all_to_all(
        serve_rows(local_rows, wanted), "row", split_axis=0, concat_axis=0, tiled=True
    )
    return (answer_rows, wanted)


def multiply(matrix, local_rows, fetched, wanted):
    owners, slots_per = wanted.shape
    group_blocks = local_rows.reshape(GROUP_BLOCK_ROWS, B, K)
    gathered = fetched.reshape(owners * slots_per, B, K)
    direct = jnp.einsum("isab,sbn->ian", matrix, gathered, preferred_element_type=jnp.float32)
    mirror = jnp.einsum("isab,ian->sbn", matrix, group_blocks, preferred_element_type=jnp.float32)
    returned = lax.all_to_all(
        mirror.reshape(owners, slots_per, B * K), "row", split_axis=0, concat_axis=0, tiled=True
    )
    chooser = (
        wanted.reshape(-1)[:, None] == jnp.arange(GROUP_BLOCK_ROWS, dtype=jnp.int32)[None, :]
    ).astype(jnp.float32)
    folded = jnp.dot(
        chooser.T,
        returned.reshape(owners * slots_per, B * K),
        precision=lax.Precision.HIGHEST,
        preferred_element_type=jnp.float32,
    )
    summed = (direct.reshape(GROUP_BLOCK_ROWS, B * K) + folded).reshape(GROUP_BLOCK_ROWS * B, K)
    return lax.psum(summed, "col").astype(jnp.bfloat16)


def per_device(density_panel, blocks, block_row, block_slot, requests):
    slot_count = requests.shape[0] * requests.shape[1]
    matrix = build_matrix(blocks, block_row, block_slot, slot_count)
    fetched, wanted = request_rows(density_panel, requests)
    first_product = multiply(matrix, density_panel, fetched, wanted)
    fetched, wanted = request_rows(first_product, requests)
    second_product = multiply(matrix, first_product, fetched, wanted)
    return (first_product, second_product)


def solution(mesh):
    in_specs = (
        P("row", None),
        P(("row", "col"), None),
        P(("row", "col")),
        P(("row", "col")),
        P(("row", "col"), None),
    )
    out_specs = (P("row", None), P("row", None))
    return jax.shard_map(
        per_device, mesh=mesh, in_specs=in_specs, out_specs=out_specs, check_vma=False
    )
```

profile of v0, /device:TPU:192, one launch (start us, length us, event | category | flops | bytes accessed | tf_op | source)
XLA Modules:
  0.0 715.5 jit_solution(738755219454881416)
XLA Ops:
  1.5 15.7 %all_to_all.30 = s32[64,1,2]{2,1,0:T(1,128)S(1)} all-to-all(s32[64,1,2]{2,1,0:T(1,128)S(1)} %copy.71), channel_id=1, replica_groups=mesh['row'=64,'col'=4] {'row'}, dimensions={0} | all-to-all | bytes 1024 | tf_op jit(solution)/shard_map/all_to_all | solution.py:27
  23.1 6.4 copy.77
  29.4 9.6 %all-to-all-start.1 = ((bf16[64,2,64,256]{3,1,2,0:T(2,128)(2,1)}), bf16[64,2,64,256]{3,1,2,0:T(2,128)(2,1)}, u32[]{:S(2)}, u32[]{:S(2)}) async-start(bf16[64,2,64,256]{3,1,2,0:T(2,128)(2,1)} %copy.77), calls=%async_computation.1 | async-start | bytes 8388608 | tf_op jit(solution)/shard_map/all_to_all | solution.py:28
  42.5 9.5 %copy.70 = bf16[384,64,64]{2,1,0:T(8,128)(2,1)} copy(bf16[384,64,64]{0,2,1:T(8,128)(2,1)S(1)} %bitcast.56) | data formatting | bytes 6291456 | tf_op jit(solution)/shard_map/reshape | solution.py:13
  52.1 6.4 broadcast_in_dim.37
  58.5 56.7 %scatter_fusion = bf16[8,128,64,64]{3,2,1,0:T(8,128)(2,1)} fusion(bf16[8,128,64,64]{3,2,1,0:T(8,128)(2,1)} %broadcast_in_dim.37, s32[384]{0:T(512)S(1)} %fusion.3, bf16[384,64,64]{2,1,0:T(8,128)(2,1)} %copy.70), kind=kCustom, calls=%fused_computation.2 | custom fusion | bytes 9440256 | tf_op jit(solution)/shard_map/scatter | solution.py:16
  115.2 13.5 %convolution_bitcast_fusion.1 = f32[128,64,256]{2,1,0:T(8,128)} fusion(bf16[8,128,64,64]{3,2,1,0:T(8,128)(2,1)} %scatter_fusion, bf16[8,64,256,1]{2,1,3,0:T(8,128)(2,1)S(1)} %bitcast.51), kind=kOutput, calls=%fused_computation.8 | convolution fusion | flops 2147483648 | bytes 17039360 | tf_op jit(solution)/shard_map/isab,ian->sbn/dot_general | solution.py:39
  128.7 10.8 %reshape.67 = f32[64,2,16384]{2,1,0:T(2,128)} reshape(f32[128,64,256]{2,1,0:T(8,128)} %convolution_bitcast_fusion.1) | data formatting | bytes 16777216 | tf_op jit(solution)/shard_map/reshape | solution.py:41
  139.5 10.6 %all-to-all-start.2 = ((f32[64,2,16384]{2,1,0:T(2,128)}), f32[64,2,16384]{2,1,0:T(2,128)}, u32[]{:S(2)}, u32[]{:S(2)}) async-start(f32[64,2,16384]{2,1,0:T(2,128)} %reshape.67), calls=%async_computation.2 | async-start | bytes 16777216 | tf_op jit(solution)/shard_map/all_to_all | solution.py:40
  154.6 7.6 %convolution_bitcast_fusion.3 = f32[1,8,64,256]{3,2,1,0:T(8,128)S(1)} fusion(bf16[8,128,64,64]{3,2,1,0:T(8,128)(2,1)} %scatter_fusion, bf16[128,64,256,1]{2,1,0,3:T(8,128)(2,1)S(1)} %bitcast.58), kind=kOutput, calls=%fused_computation.10 | convolution fusion | flops 2147483648 | bytes 13107200 | tf_op jit(solution)/shard_map/isab,sbn->ian/dot_general | solution.py:38
  162.5 170.1 %all-to-all-done.2 = f32[64,2,16384]{2,1,0:T(2,128)} async-done(((f32[64,2,16384]{2,1,0:T(2,128)}), f32[64,2,16384]{2,1,0:T(2,128)}, u32[]{:S(2)}, u32[]{:S(2)}) %all-to-all-start.2) | async-done | bytes 8388640 | tf_op jit(solution)/shard_map/all_to_all | solution.py:40
  332.6 10.9 %reshape.68 = f32[128,16384]{1,0:T(8,128)} reshape(f32[64,2,16384]{2,1,0:T(2,128)} %all-to-all-done.2) | data formatting | bytes 16777216 | tf_op jit(solution)/shard_map/reshape | solution.py:48
  348.7 22.7 %all-reduce.2 = bf16[512,256]{1,0:T(8,128)(2,1)S(1)} all-reduce(f32[512,256]{1,0:T(8,128)S(1)} %reshape.69), channel_id=1, replica_groups=mesh['row'=64,'col'=4] {'col'}, use_global_device_ids=true, to_apply=%region_1.3 | all-reduce | flops 131072 | bytes 786432 | tf_op jit(solution)/shard_map/psum | solution.py:53
  376.8 6.4 copy.83
  383.1 10.5 %all-to-all-start.3 = ((bf16[64,2,64,256]{3,1,2,0:T(2,128)(2,1)}), bf16[64,2,64,256]{3,1,2,0:T(2,128)(2,1)}, u32[]{:S(2)}, u32[]{:S(2)}) async-start(bf16[64,2,64,256]{3,1,2,0:T(2,128)(2,1)} %copy.83), calls=%async_computation.3 | async-start | bytes 8388608 | tf_op jit(solution)/shard_map/all_to_all | solution.py:28
  393.7 13.5 %convolution_bitcast_fusion = f32[128,64,256]{2,1,0:T(8,128)} fusion(bf16[8,128,64,64]{3,2,1,0:T(8,128)(2,1)} %scatter_fusion, bf16[8,64,256,1]{2,1,3,0:T(8,128)(2,1)S(1)} %bitcast.53), kind=kOutput, calls=%fused_computation.7 | convolution fusion | flops 2147483648 | bytes 17039360 | tf_op jit(solution)/shard_map/isab,ian->sbn/dot_general | solution.py:39
  407.2 10.8 %reshape.73 = f32[64,2,16384]{2,1,0:T(2,128)} reshape(f32[128,64,256]{2,1,0:T(8,128)} %convolution_bitcast_fusion) | data formatting | bytes 16777216 | tf_op jit(solution)/shard_map/reshape | solution.py:41
  418.0 68.8 %all-to-all-done.3 = bf16[64,2,64,256]{3,1,2,0:T(2,128)(2,1)} async-done(((bf16[64,2,64,256]{3,1,2,0:T(2,128)(2,1)}), bf16[64,2,64,256]{3,1,2,0:T(2,128)(2,1)}, u32[]{:S(2)}, u32[]{:S(2)}) %all-to-all-start.3) | async-done | bytes 4194336 | tf_op jit(solution)/shard_map/all_to_all | solution.py:28
  486.8 8.7 %all-to-all-start.4 = ((f32[64,2,16384]{2,1,0:T(2,128)}), f32[64,2,16384]{2,1,0:T(2,128)}, u32[]{:S(2)}, u32[]{:S(2)}) async-start(f32[64,2,16384]{2,1,0:T(2,128)} %reshape.73), calls=%async_computation.4 | async-start | bytes 16777216 | tf_op jit(solution)/shard_map/all_to_all | solution.py:40
  498.6 7.6 %convolution_bitcast_fusion.2 = f32[1,8,64,256]{3,2,1,0:T(8,128)S(1)} fusion(bf16[8,128,64,64]{3,2,1,0:T(8,128)(2,1)} %scatter_fusion, bf16[128,64,256,1]{2,1,0,3:T(8,128)(2,1)S(1)} %bitcast.57), kind=kOutput, calls=%fused_computation.9 | convolution fusion | flops 2147483648 | bytes 13107200 | tf_op jit(solution)/shard_map/isab,sbn->ian/dot_general | solution.py:38
  506.5 171.6 %all-to-all-done.4 = f32[64,2,16384]{2,1,0:T(2,128)} async-done(((f32[64,2,16384]{2,1,0:T(2,128)}), f32[64,2,16384]{2,1,0:T(2,128)}, u32[]{:S(2)}, u32[]{:S(2)}) %all-to-all-start.4) | async-done | bytes 8388640 | tf_op jit(solution)/shard_map/all_to_all | solution.py:40
  678.2 10.9 %reshape.74 = f32[128,16384]{1,0:T(8,128)} reshape(f32[64,2,16384]{2,1,0:T(2,128)} %all-to-all-done.4) | data formatting | bytes 16777216 | tf_op jit(solution)/shard_map/reshape | solution.py:48
  689.0 5.2 convolution_add_fusion
  694.3 20.9 %all-reduce.3 = bf16[512,256]{1,0:T(8,128)(2,1)} all-reduce(f32[512,256]{1,0:T(8,128)S(1)} %reshape.75), channel_id=1, replica_groups=mesh['row'=64,'col'=4] {'col'}, use_global_device_ids=true, to_apply=%region_2.4 | all-reduce | flops 131072 | bytes 786432 | tf_op jit(solution)/shard_map/psum | solution.py:53
  (38 shorter events, 29.0 us)
Async XLA Ops:
  0.6 17.1 %copy-start = (bf16[512,256]{1,0:T(8,128)(2,1)S(1)}, bf16[512,256]{1,0:T(8,128)(2,1)}, u32[]{:S(2)}) copy-start(bf16[512,256]{1,0:T(8,128)(2,1)} %param.7) | copy-start | bytes 786436
  29.4 110.1 %all-to-all-start.1 = ((bf16[64,2,64,256]{3,1,2,0:T(2,128)(2,1)}), bf16[64,2,64,256]{3,1,2,0:T(2,128)(2,1)}, u32[]{:S(2)}, u32[]{:S(2)}) async-start(bf16[64,2,64,256]{3,1,2,0:T(2,128)(2,1)} %copy.77), calls=%async_computation.1 | async-start | bytes 8388608 | tf_op jit(solution)/shard_map/all_to_all | solution.py:28
  42.5 9.6 %copy-start.3 = (s32[384]{0:T(512)S(1)}, s32[384]{0:T(512)}, u32[]{:S(2)}) copy-start(s32[384]{0:T(512)} %param.10) | copy-start | bytes 4612
  42.5 9.6 %copy-start.4 = (s32[384]{0:T(512)S(1)}, s32[384]{0:T(512)}, u32[]{:S(2)}) copy-start(s32[384]{0:T(512)} %param.9) | copy-start | bytes 4612
  139.5 193.0 %all-to-all-start.2 = ((f32[64,2,16384]{2,1,0:T(2,128)}), f32[64,2,16384]{2,1,0:T(2,128)}, u32[]{:S(2)}, u32[]{:S(2)}) async-start(f32[64,2,16384]{2,1,0:T(2,128)} %reshape.67), calls=%async_computation.2 | async-start | bytes 16777216 | tf_op jit(solution)/shard_map/all_to_all | solution.py:40
  371.4 22.2 %copy-start.2 = (bf16[512,256]{1,0:T(8,128)(2,1)}, bf16[512,256]{1,0:T(8,128)(2,1)S(1)}, u32[]{:S(2)}) copy-start(bf16[512,256]{1,0:T(8,128)(2,1)S(1)} %all-reduce.2) | copy-start | bytes 786436
  383.1 103.7 %all-to-all-start.3 = ((bf16[64,2,64,256]{3,1,2,0:T(2,128)(2,1)}), bf16[64,2,64,256]{3,1,2,0:T(2,128)(2,1)}, u32[]{:S(2)}, u32[]{:S(2)}) async-start(bf16[64,2,64,256]{3,1,2,0:T(2,128)(2,1)} %copy.83), calls=%async_computation.3 | async-start | bytes 8388608 | tf_op jit(solution)/shard_map/all_to_all | solution.py:28
  486.8 191.3 %all-to-all-start.4 = ((f32[64,2,16384]{2,1,0:T(2,128)}), f32[64,2,16384]{2,1,0:T(2,128)}, u32[]{:S(2)}, u32[]{:S(2)}) async-start(f32[64,2,16384]{2,1,0:T(2,128)} %reshape.73), calls=%async_computation.4 | async-start | bytes 16777216 | tf_op jit(solution)/shard_map/all_to_all | solution.py:40
  689.0 26.2 %copy-start.1 = (bf16[512,256]{1,0:T(8,128)(2,1)S(1)}, bf16[512,256]{1,0:T(8,128)(2,1)}, u32[]{:S(2)}) copy-start(bf16[512,256]{1,0:T(8,128)(2,1)} %param.7) | copy-start | bytes 786436
where the time goes:
time: 729 us; the launch traced here: 715 us
  waiting for transfers between devices  410 us (56%)
  local copies, waits for them, and re-layouts  147 us (20%)
  blocking collectives  59.3 us (8%)
  matrix products  52.6 us (7%)
  starting transfers between devices  39.4 us (5%)
    all_to_all x2, waiting for transfers between devices, multiply(): lax.all_to_all(mirror.reshape(owners, slots_per, B * K), 'row', split_axi...  342 us
    all_to_all x2, waiting for transfers between devices, request_rows(): lax.all_to_all(serve_rows(local_rows, wanted), 'row', split_axis=0, conca...  68.8 us
    scatter x1, local copies, waits for them, and re-layouts, build_matrix(): return zero_blocks.at[block_row, target].set(pieces, mode='drop')  56.7 us
    psum x2, blocking collectives, multiply(): return lax.psum(summed, 'col').astype(jnp.bfloat16)  43.6 us
    dot_general x2, matrix products, multiply(): jnp.einsum('isab,ian->sbn', matrix, group_blocks, preferred_element_type=...  27 us
    reshape x2, local copies, waits for them, and re-layouts, multiply(): returned.reshape(owners * slots_per, B * K)  21.8 us
    reshape x2, local copies, waits for them, and re-layouts, multiply(): mirror.reshape(owners, slots_per, B * K)  21.6 us
    all_to_all x2, starting transfers between devices, request_rows(): lax.all_to_all(serve_rows(local_rows, wanted), 'row', split_axis=0, conca...  20.2 us
  transfers between devices with their start and end apart: 4, of which 3 were waited for; matrix products, arithmetic and copies ran while one was open for 21% of the time, Pallas kernels for 0%

commit v1 on v0

v1 whole, which is shorter than its diff:
```python
import functools

import jax
import jax.numpy as jnp
from jax import lax
from jax.experimental import pallas as pl
from jax.experimental.pallas import tpu as pltpu
from jax.sharding import PartitionSpec as P

B = 64
K = 256
Z, Y, C, X = 8, 4, 2, 4
BF16, F32 = jnp.bfloat16, jnp.float32


def positions(block_row, block_slot):
    z, y, core, t = block_slot // 16, (block_slot // 4) % 4, (block_slot // 2) % 2, block_slot % 2
    place = ((z * C + core) * Y + y) * 16 + t * 8 + block_row
    return jnp.where(block_slot >= 0, place, -1).reshape(1, -1)


def kernel(
    panel, blocks, place, out1, out2,
    matrix, pick, perm, pt, gathered, acc, held, own,
    core_out, core_in, y_out, y_in, z_out, z_in, z_own, x_out, x_in,
    ay_s, ay_r, az_s, az_r, ac_s, ac_r, rc_s, rc_r, ry_s, ry_r, rz_s, rz_r, xr_s, xr_r, xg_s, xg_r,
):
    row, x = lax.axis_index("row"), lax.axis_index("col")
    z, y, k = row // (Y * C), (row // C) % Y, row % C

    def at(zz, yy, kk):
        return (zz * Y + yy) * C + kk

    def copy(src, dst, send, recv, to_row, to_col=None):
        return pltpu.make_async_remote_copy(
            src_ref=src, dst_ref=dst, send_sem=send, recv_sem=recv,
            device_id=(to_row, x if to_col is None else to_col),
            device_id_type=pl.DeviceIdType.MESH,
        )

    barrier = pltpu.get_barrier_semaphore()

    def greet(to_row, to_col):
        pl.semaphore_signal(barrier, inc=1, device_id=(to_row, to_col), device_id_type=pl.DeviceIdType.MESH)

    greet(at(z, y, 1 - k), x)
    for d in range(1, Y):
        greet(at(z, (y + d) % Y, k), x)
    for d in range(1, Z):
        greet(at((z + d) % Z, y, k), x)
    for d in range(1, X):
        greet(row, (x + d) % X)

    r = lax.broadcasted_iota(jnp.int32, (512, 384), 0)
    want = (r // 8) * 16 + r % 8
    at_place = jnp.broadcast_to(place[...], (512, 384))
    pick[:, 0:384] = jnp.where(at_place == want, 1.0, 0.0).astype(BF16)
    pick[:, 384:768] = jnp.where(at_place == want + 8, 1.0, 0.0).astype(BF16)
    j = lax.broadcasted_iota(jnp.int32, (512, 512), 0)
    q = lax.broadcasted_iota(jnp.int32, (512, 512), 1)
    i, a = j % 8, j // 8
    perm[...] = jnp.where(q == ((i % 4) * 2 + i // 4) * 64 + a, 1.0, 0.0).astype(BF16)
    for c in range(X):
        for t in range(2):
            held[0, c, t * 64:(t + 1) * 64, :] = panel[(c + 4 * t) * 64:(c + 4 * t + 1) * 64, :]

    def build(step, carry):
        tile = blocks[:, pl.ds(pl.multiple_of(step * 128, 128), 128)].astype(F32)
        turned = pltpu.roll(tile, 64, 1)
        low = lax.broadcasted_iota(jnp.int32, (384, 128), 1) < 64
        upper = jnp.concatenate([jnp.where(low, tile, 0.0), jnp.where(low, turned, 0.0)], axis=1)
        lower = jnp.concatenate([jnp.where(low, 0.0, turned), jnp.where(low, 0.0, tile)], axis=1)
        both = jnp.concatenate([upper, lower], axis=0).astype(BF16)
        placed = jnp.dot(pick[...], both, preferred_element_type=F32)
        first = placed[:, 0:128].reshape(64, 8, 128)
        second = placed[:, 128:256].reshape(64, 8, 128)
        rows = jnp.concatenate([first, second], axis=1).astype(BF16)
        for chunk in range(64):
            matrix[pl.ds(pl.multiple_of(step * 16, 16), 16), chunk * 128:(chunk + 1) * 128] = rows[chunk]
        return carry

    def ag_y(p, d):
        part = gathered.at[p, z, k, pl.ds(pl.multiple_of(y * 128, 128), 128)]
        return copy(part, part, ay_s.at[p, d - 1], ay_r.at[p, d - 1], at(z, (y + d) % Y, k))

    def ag_z(p, way, s, zo, to):
        unit = gathered.at[p, zo, k]
        return copy(unit, unit, az_s.at[p, way, s - 1], az_r.at[p, way, s - 1], at(to, y, k))

    def ag_core(p, zo):
        unit = gathered.at[p, zo, k]
        return copy(unit, unit, ac_s.at[p, zo], ac_r.at[p, zo], at(z, y, 1 - k))

    def ag_core_arrival(p, zo):
        unit = gathered.at[p, zo, 1 - k]
        return copy(unit, unit, ac_s.at[p, zo], ac_r.at[p, zo], at(z, y, 1 - k))

    def rs_core(p, zo):
        return copy(core_out.at[p, zo], core_in.at[p, zo], rc_s.at[p, zo], rc_r.at[p, zo], at(z, y, 1 - k))

    def rs_y(p, zo, d):
        to = (y + d) % Y
        return copy(y_out.at[p, zo, to], y_in.at[p, zo, d - 1], ry_s.at[p, zo, d - 1], ry_r.at[p, zo, d - 1], at(z, to, k))

    def rs_z(p, zo):
        return copy(z_out.at[p, zo], z_in.at[p, z], rz_s.at[p, zo], rz_r.at[p, z], at(zo, y, k))

    def rs_z_arrival(p, zi):
        return copy(z_out.at[p, zi], z_in.at[p, zi], rz_s.at[p, zi], rz_r.at[p, zi], at(zi, y, k))

    def rs_x(p, d):
        to = (x + d) % X
        return copy(x_out.at[p, to], x_in.at[p, d - 1], xr_s.at[p, d - 1], xr_r.at[p, d - 1], row, to)

    def ag_x(p, d):
        part = held.at[p + 1, x]
        return copy(part, part, xg_s.at[p, d - 1], xg_r.at[p, d - 1], row, (x + d) % X)

    def ag_x_arrival(p, d):
        part = held.at[p + 1, (x + X - d) % X]
        return copy(part, part, xg_s.at[p, d - 1], xg_r.at[p, d - 1], row, (x + d) % X)

    def down_sends(s):
        return (z >= 1) & (z + s - 1 <= 7) & (s <= 4 - k), z + s - 1, z - 1

    def down_gets(s):
        return (z + s <= 7) & (s <= 4 - k), z + s

    def up_sends(s):
        zo = (z + 8 - (s - 1)) % 8
        return (zo >= 5 - k) & (s <= 3 + k), zo, (z + 1) % 8

    def up_gets(s):
        zo = (z + 8 - s) % 8
        return (zo >= 5 - k) & (s <= 3 + k), zo

    def columns(zo, kk):
        return pl.ds(pl.multiple_of((zo * C + kk) * 512, 512), 512)

    def direct(p, zo, kk):
        part = jnp.dot(matrix[:, columns(zo, kk)], gathered[p, zo, kk], preferred_element_type=F32)
        for half in range(2):
            acc[half] += part[:, half * 128:(half + 1) * 128]

    def ag_start(p):
        gathered[p, z, k, pl.ds(pl.multiple_of(y * 128, 128), 128), :] = held[p, x]
        for d in range(1, Y):
            ag_y(p, d).start()

    def ag_pass(p, s):
        cond, zo, to = down_sends(s)

        @pl.when(cond)
        def _():
            ag_z(p, 0, s, zo, to).start()

        cond, zo, to = up_sends(s)

        @pl.when(cond)
        def _():
            ag_z(p, 1, s, zo, to).start()

    def ag_wait(p, s):
        cond, zo = down_gets(s)

        @pl.when(cond)
        def _():
            ag_z(p, 0, s, zo, z).wait_recv()

        cond, zo = up_gets(s)

        @pl.when(cond)
        def _():
            ag_z(p, 1, s, zo, z).wait_recv()

    def ag_use(p, s):
        cond, zo = down_gets(s)

        @pl.when(cond)
        def _():
            ag_core(p, zo).start()
            direct(p, zo, k)

        cond, zo = up_gets(s)

        @pl.when(cond & (zo > z))
        def _():
            ag_core(p, zo).start()
            direct(p, zo, k)

    def ag_first(p):
        for d in range(1, Y):
            ag_y(p, d).wait_recv()
        ag_pass(p, 1)
        ag_core(p, z).start()

    def ag_step(p, s):
        ag_wait(p, s)
        if s < 4:
            ag_pass(p, s + 1)
        ag_use(p, s)

    def others(p):
        def use(zo, carry):
            ag_core_arrival(p, zo).wait_recv()
            direct(p, zo, 1 - k)
            return carry

        lax.fori_loop(z, Z, use, 0)

    def make_pt(p):
        ordered = jnp.dot(perm[...], held[p].reshape(512, 256), preferred_element_type=F32)
        pt[...] = ordered.T.astype(BF16)

    def mirror(zo, kk):
        return jnp.dot(pt[...], matrix[:, columns(zo, kk)], preferred_element_type=F32)

    def rs_a(p):
        def send(step, carry):
            zo = 7 - step
            core_out[p, zo] = mirror(zo, 1 - k).astype(BF16)
            rs_core(p, zo).start()
            return carry

        lax.fori_loop(0, Z - z, send, 0)

    def rs_b(p):
        def send(step, carry):
            zo = 7 - step
            part = mirror(zo, k)
            rs_core(p, zo).wait_recv()
            part = part + core_in[p, zo].astype(F32)
            for to in range(Y):
                piece = part[:, to * 128:(to + 1) * 128]
                own[zo, to] = piece
                y_out[p, zo, to] = piece.astype(BF16)
            for d in range(1, Y):
                rs_y(p, zo, d).start()
            return carry

        lax.fori_loop(0, Z - z, send, 0)

    def rs_c(p, zo):
        @pl.when(zo >= z)
        def _():
            total = own[zo, y]
            for d in range(1, Y):
                rs_y(p, zo, d).wait_recv()
                total = total + y_in[p, zo, d - 1].astype(F32)

            @pl.when(zo > z)
            def _():
                z_out[p, zo] = total.astype(BF16)
                rs_z(p, zo).start()

            @pl.when(zo == z)
            def _():
                z_own[...] = total

    def rs_d(p):
        def add(zi, carry):
            rs_z_arrival(p, zi).wait_recv()
            z_own[...] += z_in[p, zi].astype(F32)
            return carry

        lax.fori_loop(0, z, add, 0)

    def x_start(p):
        for c in range(X):
            for t in range(2):
                for half in range(2):
                    x_out[p, c, t * 64:(t + 1) * 64, half * 128:(half + 1) * 128] = acc[
                        half, pl.ds(c + 4 * t, 64, stride=8), :
                    ]
        for d in range(1, X):
            rs_x(p, d).start()

    def finish(p, out):
        total = x_out[p, x] + z_own[...].T
        for d in range(1, X):
            rs_x(p, d).wait_recv()
            total = total + x_in[p, d - 1]
        held[p + 1, x] = total.astype(BF16)
        for d in range(1, X):
            ag_x(p, d).start()

    def collect(p, out):
        for d in range(1, X):
            ag_x_arrival(p, d).wait_recv()
        for c in range(X):
            for t in range(2):
                out[(c + 4 * t) * 64:(c + 4 * t + 1) * 64, :] = held[p + 1, c, t * 64:(t + 1) * 64, :]

    def product(p, out):
        acc[...] = jnp.zeros_like(acc)
        if p == 0:
            lax.fori_loop(0, 12, build, 0)
            ag_first(p)
            lax.fori_loop(12, 32, build, 0)
        make_pt(p)
        rs_a(p)
        if p == 1:
            ag_first(p)
        rs_b(p)
        direct(p, z, k)
        ag_step(p, 1)
        rs_c(p, 7)
        rs_c(p, 6)
        ag_step(p, 2)
        rs_c(p, 5)
        rs_c(p, 4)
        ag_step(p, 3)
        rs_c(p, 3)
        rs_c(p, 2)
        ag_step(p, 4)
        others(p)
        x_start(p)
        rs_c(p, 1)
        rs_c(p, 0)
        rs_d(p)
        finish(p, out)

    pl.semaphore_wait(barrier, 1 + (Y - 1) + (Z - 1) + (X - 1))
    ag_start(0)
    product(0, out1)
    ag_start(1)
    collect(0, out1)
    product(1, out2)
    collect(1, out2)

    for p in range(2):
        for d in range(1, Y):
            ag_y(p, d).wait_send()
        for d in range(1, X):
            rs_x(p, d).wait_send()
            ag_x(p, d).wait_send()
        for s in range(1, 5):
            cond, zo, to = down_sends(s)

            @pl.when(cond)
            def _():
                ag_z(p, 0, s, zo, to).wait_send()

            cond, zo, to = up_sends(s)

            @pl.when(cond)
            def _():
                ag_z(p, 1, s, zo, to).wait_send()

        def left(zo, carry):
            ag_core(p, zo).wait_send()
            rs_core(p, zo).wait_send()
            for d in range(1, Y):
                rs_y(p, zo, d).wait_send()

            @pl.when(zo > z)
            def _():
                rs_z(p, zo).wait_send()

            return carry

        lax.fori_loop(z, Z, left, 0)


def per_device(density_panel, blocks, block_row, block_slot, requests):
    vmem = pl.BlockSpec(memory_space=pltpu.VMEM)
    dma = pltpu.SemaphoreType.DMA
    shape = jax.ShapeDtypeStruct((512, K), BF16)
    scratch = [
        pltpu.VMEM((512, 8192), BF16),
        pltpu.VMEM((512, 768), BF16),
        pltpu.VMEM((512, 512), BF16),
        pltpu.VMEM((256, 512), BF16),
        pltpu.VMEM((2, Z, C, 512, K), BF16),
        pltpu.VMEM((2, 512, 128), F32),
        pltpu.VMEM((3, X, 128, K), BF16),
        pltpu.VMEM((Z, Y, K, 128), F32),
        pltpu.VMEM((2, Z, K, 512), BF16),
        pltpu.VMEM((2, Z, K, 512), BF16),
        pltpu.VMEM((2, Z, Y, K, 128), BF16),
        pltpu.VMEM((2, Z, Y - 1, K, 128), BF16),
        pltpu.VMEM((2, Z, K, 128), BF16),
        pltpu.VMEM((2, Z, K, 128), BF16),
        pltpu.VMEM((K, 128), F32),
        pltpu.VMEM((2, X, 128, K), F32),
        pltpu.VMEM((2, X - 1, 128, K), F32),
        dma((2, Y - 1)), dma((2, Y - 1)),
        dma((2, 2, 4)), dma((2, 2, 4)),
        dma((2, Z)), dma((2, Z)),
        dma((2, Z)), dma((2, Z)),
        dma((2, Z, Y - 1)), dma((2, Z, Y - 1)),
        dma((2, Z)), dma((2, Z)),
        dma((2, X - 1)), dma((2, X - 1)),
        dma((2, X - 1)), dma((2, X - 1)),
    ]
    return pl.pallas_call(
        kernel,
        out_shape=(shape, shape),
        in_specs=[vmem, vmem, vmem],
        out_specs=(vmem, vmem),
        scratch_shapes=scratch,
        compiler_params=pltpu.CompilerParams(
            collective_id=0, has_side_effects=True, vmem_limit_bytes=60 * 1024 * 1024
        ),
    )(density_panel, blocks, positions(block_row, block_slot))


def solution(mesh):
    in_specs = (
        P("row", None),
        P(("row", "col"), None),
        P(("row", "col")),
        P(("row", "col")),
        P(("row", "col"), None),
    )
    out_specs = (P("row", None), P("row", None))
    return jax.shard_map(
        per_device, mesh=mesh, in_specs=in_specs, out_specs=out_specs, check_vma=False
    )
```

time: 729 us -> 123 us (0.17)
  the two profiles are of different devices: /device:TPU:192 before, /device:TPU:48 now
where the time goes in v1:
time: 123 us
  Pallas kernels  118 us (96%)
  local copies, waits for them, and re-layouts  3.9 us (3%)
    pallas_call x1, Pallas kernels, per_device(): pl.pallas_call(kernel, out_shape=(shape, shape), in_specs=[vmem, vmem, vm...  118 us
    unnamed x2, local copies, waits for them, and re-layouts  3.34 us

profile of v1, /device:TPU:48, one launch (start us, length us, event | category | flops | bytes accessed | tf_op | source)
XLA Modules:
  0.0 123.3 jit_solution(4901551351459828713)
XLA Ops:
  0.6 0.7 compare_select_fusion
  1.4 0.6 reshape.7.place
  1.9 118.0 %shard_map.59 = (bf16[512,256]{1,0:T(8,128)(2,1)}, bf16[512,256]{1,0:T(8,128)(2,1)}) custom-call(bf16[512,256]{1,0:T(8,128)(2,1)} %panel.1, bf16[384,4096]{1,0:T(8,128)(2,1)} %blocks.1, s32[1,384]{1,0:T(1,128)} %reshape.7.place), custom_call_target="tpu_custom_call" | custom-call | tf_op jit(solution)/shard_map/pallas_call | solution.py:396
  119.9 1.7 %copy.8 = bf16[512,256]{1,0:T(8,128)(2,1)} copy(bf16[512,256]{1,0:T(8,128)(2,1)} %get-tuple-element.4) | data formatting | bytes 524288
  121.6 1.7 %copy.9 = bf16[512,256]{1,0:T(8,128)(2,1)} copy(bf16[512,256]{1,0:T(8,128)(2,1)} %get-tuple-element.5) | data formatting | bytes 524288

commit v2 on v0

v2 whole, which is shorter than its diff:
```python
import jax
import jax.numpy as jnp
from jax import lax
from jax.experimental import pallas as pl
from jax.experimental.pallas import tpu as pltpu
from jax.sharding import PartitionSpec as P

B = 64
K = 256
Z, Y, C, X = 8, 4, 2, 4
BF16, F32 = jnp.bfloat16, jnp.float32
RELAY, SUMMED, DIRECT = 0, 1, 2
BUILDS, FIRST_AFTER, STEP_AFTER = 16, 3, (9, 12, 15)


def kernel(
    panel, blocks, block_row, block_slot, out,
    stored, matrix, pick, perm, pt, gathered, acc, held, own,
    core_out, core_in, y_out, y_in, z_out, z_in, z_own, x_out, x_in,
    fetch, ay_s, ay_r, az_s, az_r, ac_s, ac_r, rc_s, rc_r, ry_s, ry_r, rz_s, rz_r, xr_s, xr_r, xg_s, xg_r,
):
    row, x = lax.axis_index("row"), lax.axis_index("col")
    z, y, k = row // (Y * C), (row // C) % Y, row % C
    ahead, behind, across = (y + 1 + 2 * k) % Y, (y + 3 + 2 * k) % Y, (y + 2) % Y

    def at(zz, yy, kk):
        return (zz * Y + yy) * C + kk

    def copy(src, dst, send, recv, to_row, to_col=None):
        return pltpu.make_async_remote_copy(
            src_ref=src, dst_ref=dst, send_sem=send, recv_sem=recv,
            device_id=(to_row, x if to_col is None else to_col),
            device_id_type=pl.DeviceIdType.MESH,
        )

    def load(part):
        lanes = pl.ds(pl.multiple_of(part * 1024, 1024), 1024)
        return pltpu.make_async_copy(blocks.at[:, lanes], stored.at[:, lanes], fetch.at[part])

    for part in range(4):
        load(part).start()
    barrier = pltpu.get_barrier_semaphore()

    def greet(to_row, to_col):
        pl.semaphore_signal(barrier, inc=1, device_id=(to_row, to_col), device_id_type=pl.DeviceIdType.MESH)

    greet(at(z, y, 1 - k), x)
    for d in range(1, Y):
        greet(at(z, (y + d) % Y, k), x)
    for d in range(1, Z):
        greet(at((z + d) % Z, y, k), x)
    for d in range(1, X):
        greet(row, (x + d) % X)

    for h in range(2):
        for c in range(X):
            for t in range(2):
                held[0, h, c, t * 64:(t + 1) * 64, :] = panel[
                    (c + 4 * t) * 64:(c + 4 * t + 1) * 64, h * 128:(h + 1) * 128
                ]

    def set_up():
        slot = block_slot[...]
        chunk_of = ((slot // 16) * C + (slot // 2) % 2) * Y + (slot // 4) % 4
        place = jnp.where(slot >= 0, chunk_of * 16 + (slot % 2) * 8 + block_row[...], -1)
        r = lax.broadcasted_iota(jnp.int32, (512, 384), 0)
        want = (r // 8) * 16 + r % 8
        at_place = jnp.broadcast_to(place, (512, 384))
        pick[:, 0:384] = jnp.where(at_place == want, 1.0, 0.0).astype(BF16)
        pick[:, 384:768] = jnp.where(at_place == want + 8, 1.0, 0.0).astype(BF16)
        j = lax.broadcasted_iota(jnp.int32, (512, 512), 0)
        q = lax.broadcasted_iota(jnp.int32, (512, 512), 1)
        i, a = j % 8, j // 8
        perm[...] = jnp.where(q == ((i % 4) * 2 + i // 4) * 64 + a, 1.0, 0.0).astype(BF16)

    def build(step):
        tile = stored[:, pl.ds(pl.multiple_of(step * 128, 128), 128)].astype(F32)
        turned = pltpu.roll(tile, 64, 1)
        low = lax.broadcasted_iota(jnp.int32, (384, 128), 1) < 64
        upper = jnp.concatenate([jnp.where(low, tile, 0.0), jnp.where(low, turned, 0.0)], axis=1)
        lower = jnp.concatenate([jnp.where(low, 0.0, turned), jnp.where(low, 0.0, tile)], axis=1)
        both = jnp.concatenate([upper, lower], axis=0).astype(BF16)
        placed = jnp.dot(pick[...], both, preferred_element_type=F32)
        first = placed[:, 0:128].reshape(64, 8, 128)
        second = placed[:, 128:256].reshape(64, 8, 128)
        rows = jnp.concatenate([first, second], axis=1).astype(BF16)
        for chunk in range(64):
            matrix[pl.ds(pl.multiple_of(step * 16, 16), 16), chunk * 128:(chunk + 1) * 128] = rows[chunk]

    def ag_y(p, h, d):
        part = gathered.at[p, h, z, k, pl.ds(pl.multiple_of(y * 128, 128), 128)]
        return copy(part, part, ay_s.at[p, h, d - 1], ay_r.at[p, h, d - 1], at(z, (y + d) % Y, k))

    def ag_z(p, h, way, s, zo, to):
        unit = gathered.at[p, h, zo, k]
        return copy(unit, unit, az_s.at[p, h, way, s - 1], az_r.at[p, h, way, s - 1], at(to, y, k))

    def ag_core(p, h, zo, kk):
        unit = gathered.at[p, h, zo, kk]
        return copy(unit, unit, ac_s.at[p, h, zo], ac_r.at[p, h, zo], at(z, y, 1 - k))

    def rs_core(p, zo):
        return copy(core_out.at[p, zo], core_in.at[p, zo], rc_s.at[p, zo], rc_r.at[p, zo], at(z, y, 1 - k))

    def rs_y(p, zo, what):
        to = behind if what == DIRECT else ahead
        return copy(y_out.at[p, zo, what], y_in.at[p, zo, what], ry_s.at[p, zo, what], ry_r.at[p, zo, what], at(z, to, k))

    def rs_z(p, zo, frm):
        return copy(z_out.at[p, zo], z_in.at[p, frm], rz_s.at[p, zo], rz_r.at[p, frm], at(zo, y, k))

    def rs_x(p, h, d):
        to = (x + d) % X
        return copy(x_out.at[p, h, to], x_in.at[p, h, d - 1], xr_s.at[p, h, d - 1], xr_r.at[p, h, d - 1], row, to)

    def ag_x(p, h, d, frm):
        part = held.at[p + 1, h, frm]
        return copy(part, part, xg_s.at[p, h, d - 1], xg_r.at[p, h, d - 1], row, (x + d) % X)

    def ring_send(way, s):
        down = (z >= 1) & (z + s - 1 <= 7) & (s <= 4 - k)
        up_zo = (z + 9 - s) % 8
        up = (up_zo >= 5 - k) & (s <= 3 + k)
        if way == 0:
            return down, z + s - 1, z - 1
        return up, up_zo, (z + 1) % 8

    def ring_get(way, s, kk):
        if way == 0:
            return (z + s <= 7) & (s <= 4 - kk), z + s
        zo = (z + 8 - s) % 8
        return (zo >= 5 - kk) & (s <= 3 + kk), zo

    def columns(zo, kk):
        return pl.ds(pl.multiple_of((zo * C + kk) * 512, 512), 512)

    def direct_both(p, zo, kk):
        wide = jnp.concatenate([gathered[p, 0, zo, kk], gathered[p, 1, zo, kk]], axis=1)
        part = jnp.dot(matrix[:, columns(zo, kk)], wide, preferred_element_type=F32)
        for h in range(2):
            acc[h] += part[:, h * 128:(h + 1) * 128]

    def direct_half(p, h, zo, kk):
        acc[h] += jnp.dot(matrix[:, columns(zo, kk)], gathered[p, h, zo, kk], preferred_element_type=F32)

    def ag_start(p, h):
        gathered[p, h, z, k, pl.ds(pl.multiple_of(y * 128, 128), 128), :] = held[p, h, x]
        for d in range(1, Y):
            ag_y(p, h, d).start()

    def ag_pass(p, h, s):
        for way in range(2):
            cond, zo, to = ring_send(way, s)

            @pl.when(cond)
            def _():
                ag_z(p, h, way, s, zo, to).start()

    def ag_first(p, h):
        for d in range(1, Y):
            ag_y(p, h, d).wait_recv()
        ag_pass(p, h, 1)
        ag_core(p, h, z, k).start()

    def ag_own(p):
        acc[...] = jnp.zeros_like(acc)

        def use(kk, carry):
            @pl.when(kk != k)
            def _():
                for h in range(2):
                    ag_core(p, h, z, kk).wait_recv()

            direct_both(p, z, kk)
            return carry

        lax.fori_loop(0, C, use, 0)

    def ag_step(p, e):
        s, h = 1 + e // 2, e % 2
        for way in range(2):
            cond, zo = ring_get(way, s, k)

            @pl.when(cond)
            def _():
                ag_z(p, h, way, s, zo, z).wait_recv()

        @pl.when(s < 4)
        def _():
            ag_pass(p, h, s + 1)

        for way in range(2):
            cond, zo = ring_get(way, s, k)

            @pl.when(cond & (zo > z))
            def _():
                ag_core(p, h, zo, k).start()

    def ag_use(p, e, mine):
        s, h = 1 + e // 2, e % 2

        def use(way, carry):
            kk = k if mine else 1 - k
            down, zd = ring_get(0, s, kk)
            up, zu = ring_get(1, s, kk)
            zo = jnp.where(way == 0, zd, zu)
            cond = ((way == 0) & down | (way == 1) & up) & (zo > z)

            @pl.when(cond)
            def _():
                if not mine:
                    ag_core(p, h, zo, kk).wait_recv()

                @pl.when(s == 4)
                def _():
                    direct_half(p, h, zo, kk)

                @pl.when((s < 4) & (h == 1))
                def _():
                    direct_both(p, zo, kk)

            return carry

        lax.fori_loop(0, 2, use, 0)

    def make_pt(p):
        for h in range(2):
            ordered = jnp.dot(perm[...], held[p, h].reshape(512, 128), preferred_element_type=F32)
            pt[h * 128:(h + 1) * 128, :] = ordered.T.astype(BF16)

    def mirror(zo, kk):
        return jnp.dot(pt[...], matrix[:, columns(zo, kk)], preferred_element_type=F32)

    def rs_a(p, zo):
        core_out[p, zo] = mirror(zo, 1 - k).astype(BF16)
        rs_core(p, zo).start()

    def rs_b1(p, zo):
        part = mirror(zo, k)
        rs_core(p, zo).wait_recv()
        part = part + core_in[p, zo].astype(F32)
        for to in range(Y):
            own[zo, to] = part[:, to * 128:(to + 1) * 128]
        y_out[p, zo, RELAY] = own[zo, across].astype(BF16)
        rs_y(p, zo, RELAY).start()
        y_out[p, zo, DIRECT] = own[zo, behind].astype(BF16)
        rs_y(p, zo, DIRECT).start()

    def rs_b2(p, zo):
        rs_y(p, zo, RELAY).wait_recv()
        y_out[p, zo, SUMMED] = (own[zo, ahead] + y_in[p, zo, RELAY].astype(F32)).astype(BF16)
        rs_y(p, zo, SUMMED).start()

    def rs_c(p, zo):
        rs_y(p, zo, DIRECT).wait_recv()
        rs_y(p, zo, SUMMED).wait_recv()
        total = own[zo, y] + y_in[p, zo, DIRECT].astype(F32) + y_in[p, zo, SUMMED].astype(F32)

        @pl.when(zo > z)
        def _():
            z_out[p, zo] = total.astype(BF16)

            @pl.when(jnp.logical_not(waits(zo)))
            def _():
                rs_z(p, zo, z).start()

        @pl.when(zo == z)
        def _():
            z_own[...] = total

    def waits(zo):
        return (z >= 1) & (zo - z >= 4)

    def rs_late(p):
        for zo in range(5, Z):
            @pl.when(waits(zo))
            def _():
                rs_z(p, zo, z).start()

    def rs_d(p):
        def add(zi, carry):
            rs_z(p, zi, zi).wait_recv()
            z_own[...] += z_in[p, zi].astype(F32)
            return carry

        lax.fori_loop(0, z, add, 0)

    def x_start(p, h):
        for c in range(X):
            for t in range(2):
                x_out[p, h, c, t * 64:(t + 1) * 64, :] = acc[h, pl.ds(c + 4 * t, 64, stride=8), :]
        for d in range(1, X):
            rs_x(p, h, d).start()

    def finish(p, h):
        total = x_out[p, h, x] + z_own[h * 128:(h + 1) * 128, :].T
        for d in range(1, X):
            rs_x(p, h, d).wait_recv()
            total = total + x_in[p, h, d - 1]
        held[p + 1, h, x] = total.astype(BF16)
        for d in range(1, X):
            ag_x(p, h, d, x).start()

    def collect(p):
        for h in range(2):
            for d in range(1, X):
                ag_x(p, h, d, (x + X - d) % X).wait_recv()
        out[p] = held[p + 1]

    def product(p, carry):
        for h in range(2):
            ag_start(p, h)

        @pl.when(p == 0)
        def _():
            set_up()

            def build_some(part, carry):
                @pl.when(part % (BUILDS // 4) == 0)
                def _():
                    load(part // (BUILDS // 4)).wait()

                for n in range(32 // BUILDS):
                    build(part * (32 // BUILDS) + n)

                @pl.when(part == FIRST_AFTER)
                def _():
                    for h in range(2):
                        ag_first(p, h)

                for e, after in enumerate(STEP_AFTER):
                    @pl.when(part == after)
                    def _():
                        ag_step(p, e)

                return carry

            lax.fori_loop(0, BUILDS, build_some, 0)

        @pl.when(p == 1)
        def _():
            for h in range(2):
                ag_first(p, h)
            collect(0)

        make_pt(p)
        lead = jnp.where(p == 0, -3, 0)

        def turn(step, carry):
            n = step - 6

            def stage(first, body, count=8, skip=0):
                @pl.when((n >= first + skip) & (n < first + count))
                def _():
                    body(n - first)

            def stage_zo(first, body):
                zo = 7 - (n - first)

                @pl.when((n >= first) & (zo >= z))
                def _():
                    body(p, zo)

            stage_zo(-3, rs_a)
            stage_zo(-2, rs_b1)
            stage(lead, lambda e: ag_step(p, e), 8, jnp.where(p == 0, len(STEP_AFTER), 0))
            stage_zo(0, rs_b2)
            stage_zo(3, rs_c)
            stage(jnp.where(p == 0, -6, -1), lambda e: ag_own(p), 1)
            stage(lead, lambda e: ag_use(p, e, True))
            stage(lead + 1, lambda e: ag_use(p, e, False))
            stage(lead + 7, lambda e: x_start(p, e), 2)
            stage(jnp.where(p == 0, 6, 8), lambda e: rs_late(p), 1)
            return carry

        lax.fori_loop(0, 17, turn, 0)
        rs_d(p)
        for h in range(2):
            finish(p, h)
        return carry

    pl.semaphore_wait(barrier, 1 + (Y - 1) + (Z - 1) + (X - 1))
    lax.fori_loop(0, 2, product, 0)
    collect(1)

    def left(p, carry):
        for h in range(2):
            for d in range(1, Y):
                ag_y(p, h, d).wait_send()
            for d in range(1, X):
                rs_x(p, h, d).wait_send()
                ag_x(p, h, d, x).wait_send()
            for way in range(2):
                for s in range(1, 5):
                    cond, zo, to = ring_send(way, s)

                    @pl.when(cond)
                    def _():
                        ag_z(p, h, way, s, zo, to).wait_send()

        def left_zo(zo, carry):
            for h in range(2):
                ag_core(p, h, zo, k).wait_send()
            rs_core(p, zo).wait_send()
            for what in (RELAY, SUMMED, DIRECT):
                rs_y(p, zo, what).wait_send()

            @pl.when(zo > z)
            def _():
                rs_z(p, zo, z).wait_send()

            return carry

        lax.fori_loop(z, Z, left_zo, 0)
        return carry

    lax.fori_loop(0, 2, left, 0)


def lay_out(held, out1, out2):
    for p, out in enumerate((out1, out2)):
        for h in range(2):
            for c in range(X):
                for t in range(2):
                    out[(c + 4 * t) * 64:(c + 4 * t + 1) * 64, h * 128:(h + 1) * 128] = held[
                        p, h, c, t * 64:(t + 1) * 64, :
                    ]


def per_device(density_panel, blocks, block_row, block_slot, requests):
    vmem = pl.BlockSpec(memory_space=pltpu.VMEM)
    dma = pltpu.SemaphoreType.DMA
    shape = jax.ShapeDtypeStruct((512, K), BF16)

    def pair(*dims):
        return [dma(dims), dma(dims)]

    scratch = [
        pltpu.VMEM((384, 4096), BF16),
        pltpu.VMEM((512, 8192), BF16),
        pltpu.VMEM((512, 768), BF16),
        pltpu.VMEM((512, 512), BF16),
        pltpu.VMEM((256, 512), BF16),
        pltpu.VMEM((2, 2, Z, C, 512, 128), BF16),
        pltpu.VMEM((2, 512, 128), F32),
        pltpu.VMEM((3, 2, X, 128, 128), BF16),
        pltpu.VMEM((Z, Y, K, 128), F32),
        pltpu.VMEM((2, Z, K, 512), BF16),
        pltpu.VMEM((2, Z, K, 512), BF16),
        pltpu.VMEM((2, Z, 3, K, 128), BF16),
        pltpu.VMEM((2, Z, 3, K, 128), BF16),
        pltpu.VMEM((2, Z, K, 128), BF16),
        pltpu.VMEM((2, Z, K, 128), BF16),
        pltpu.VMEM((K, 128), F32),
        pltpu.VMEM((2, 2, X, 128, 128), F32),
        pltpu.VMEM((2, 2, X - 1, 128, 128), F32),
        dma((4,)),
        *pair(2, 2, Y - 1),
        *pair(2, 2, 2, 4),
        *pair(2, 2, Z),
        *pair(2, Z),
        *pair(2, Z, 3),
        *pair(2, Z),
        *pair(2, 2, X - 1),
        *pair(2, 2, X - 1),
    ]
    held = pl.pallas_call(
        kernel,
        out_shape=jax.ShapeDtypeStruct((2, 2, X, 128, 128), BF16),
        in_specs=[vmem, pl.BlockSpec(memory_space=pl.ANY), vmem, vmem],
        out_specs=vmem,
        scratch_shapes=scratch,
        compiler_params=pltpu.CompilerParams(
            collective_id=0, has_side_effects=True, vmem_limit_bytes=60 * 1024 * 1024
        ),
    )(density_panel, blocks, block_row, block_slot)
    return pl.pallas_call(
        lay_out, out_shape=(shape, shape), in_specs=[vmem], out_specs=(vmem, vmem)
    )(held)


def solution(mesh):
    in_specs = (
        P("row", None),
        P(("row", "col"), None),
        P(("row", "col")),
        P(("row", "col")),
        P(("row", "col"), None),
    )
    out_specs = (P("row", None), P("row", None))
    return jax.shard_map(
        per_device, mesh=mesh, in_specs=in_specs, out_specs=out_specs, check_vma=False
    )
```

time: 729 us -> 104 us (0.14); the launches traced: 715 us -> 103 us
  waiting for transfers between devices: 410 us -> 0 us
  local copies, waits for them, and re-layouts: 147 us -> 0 us
  Pallas kernels: 0 us -> 103 us
  blocking collectives: 59.3 us -> 0 us
  matrix products: 52.6 us -> 0 us
  starting transfers between devices: 39.4 us -> 0 us
    all_to_all x4 -> x0, waiting for transfers between devices: 410 us -> none  [the longest x2 342 us: multiply(): lax.all_to_all(mirror.reshape(owners, slots_per, B * K), 'row', split_axi...]
    pallas_call x0 -> x2, Pallas kernels: none -> 103 us  [the longest x1 101 us: per_device(): pl.pallas_call(kernel, out_shape=jax.ShapeDtypeStruct((2, 2, X, 128, 128)...]
    scatter x1 -> x0, local copies, waits for them, and re-layouts: 56.7 us -> none  [build_matrix(): return zero_blocks.at[block_row, target].set(pieces, mode='drop')]
    reshape x7 -> x0, local copies, waits for them, and re-layouts: 53 us -> none  [the longest x2 21.8 us: multiply(): returned.reshape(owners * slots_per, B * K)]
    dot_general x6 -> x0, matrix products: 52.6 us -> none  [the longest x2 27 us: multiply(): jnp.einsum('isab,ian->sbn', matrix, group_blocks, preferred_element_type=...]
    psum x2 -> x0, blocking collectives: 43.6 us -> none  [multiply(): return lax.psum(summed, 'col').astype(jnp.bfloat16)]
    all_to_all x4 -> x0, starting transfers between devices: 39.4 us -> none  [the longest x2 20.2 us: request_rows(): lax.all_to_all(serve_rows(local_rows, wanted), 'row', split_axis=0, conca...]
    all_to_all x1 -> x0, blocking collectives: 15.7 us -> none  [request_rows(): lax.all_to_all(requests, 'row', split_axis=0, concat_axis=0, tiled=True)]
  transfers between devices with their start and end apart: 4 -> 0, of which waited for: 3 -> 0; matrix products, arithmetic and copies ran while one was open for 21% -> 0% of each run, Pallas kernels for 0% -> 0%
where the time goes in v2:
time: 104 us; the launch traced here: 103 us
  Pallas kernels  103 us (99%)
    pallas_call x1, Pallas kernels, per_device(): pl.pallas_call(kernel, out_shape=jax.ShapeDtypeStruct((2, 2, X, 128, 128)...  101 us

profile of v2, /device:TPU:192, one launch (start us, length us, event | category | flops | bytes accessed | tf_op | source)
XLA Modules:
  0.0 103.4 jit_solution(15886905438817435527)
XLA Ops:
  0.6 100.9 %shard_map.59.held = bf16[2,2,4,128,128]{4,3,2,1,0:T(8,128)(2,1)} custom-call(bf16[512,256]{1,0:T(8,128)(2,1)} %panel.1, bf16[384,4096]{1,0:T(8,128)(2,1)} %blocks.1, s32[384]{0:T(512)} %block_row.1, s32[384]{0:T(512)} %block_slot.1), custom_call_target="tpu_custom_call" | custom-call | tf_op jit(solution)/shard_map/pallas_call | solution.py:467
  101.5 1.9 %shard_map.60 = (bf16[512,256]{1,0:T(8,128)(2,1)}, bf16[512,256]{1,0:T(8,128)(2,1)}) custom-call(bf16[2,2,4,128,128]{4,3,2,1,0:T(8,128)(2,1)} %shard_map.59.held), custom_call_target="tpu_custom_call" | custom-call | tf_op jit(solution)/shard_map/pallas_call | solution.py:477

commit v3 on v2

--- a/solution.py
+++ b/solution.py
@@ -10,14 +10,14 @@
 Z, Y, C, X = 8, 4, 2, 4
 BF16, F32 = jnp.bfloat16, jnp.float32
 RELAY, SUMMED, DIRECT = 0, 1, 2
-BUILDS, FIRST_AFTER, STEP_AFTER = 16, 3, (9, 12, 15)
+FIRST_AFTER = 3
 
 
 def kernel(
     panel, blocks, block_row, block_slot, out,
     stored, matrix, pick, perm, pt, gathered, acc, held, own,
     core_out, core_in, y_out, y_in, z_out, z_in, z_own, x_out, x_in,
-    fetch, ay_s, ay_r, az_s, az_r, ac_s, ac_r, rc_s, rc_r, ry_s, ry_r, rz_s, rz_r, xr_s, xr_r, xg_s, xg_r,
+    fetch, ay_s, ay_r, az_s, az_r, af_s, af_r, ag_s, ag_r, ac_s, ac_r, rc_s, rc_r, ry_s, ry_r, rz_s, rz_r, xr_s, xr_r, xg_s, xg_r,
 ):
     row, x = lax.axis_index("row"), lax.axis_index("col")
     z, y, k = row // (Y * C), (row // C) % Y, row % C
@@ -73,19 +73,20 @@
         i, a = j % 8, j // 8
         perm[...] = jnp.where(q == ((i % 4) * 2 + i // 4) * 64 + a, 1.0, 0.0).astype(BF16)
 
-    def build(step):
+    def build(step, half):
         tile = stored[:, pl.ds(pl.multiple_of(step * 128, 128), 128)].astype(F32)
         turned = pltpu.roll(tile, 64, 1)
         low = lax.broadcasted_iota(jnp.int32, (384, 128), 1) < 64
         upper = jnp.concatenate([jnp.where(low, tile, 0.0), jnp.where(low, turned, 0.0)], axis=1)
         lower = jnp.concatenate([jnp.where(low, 0.0, turned), jnp.where(low, 0.0, tile)], axis=1)
         both = jnp.concatenate([upper, lower], axis=0).astype(BF16)
-        placed = jnp.dot(pick[...], both, preferred_element_type=F32)
-        first = placed[:, 0:128].reshape(64, 8, 128)
-        second = placed[:, 128:256].reshape(64, 8, 128)
+        placed = jnp.dot(pick[half * 256:(half + 1) * 256, :], both, preferred_element_type=F32)
+        first = placed[:, 0:128].reshape(32, 8, 128)
+        second = placed[:, 128:256].reshape(32, 8, 128)
         rows = jnp.concatenate([first, second], axis=1).astype(BF16)
-        for chunk in range(64):
-            matrix[pl.ds(pl.multiple_of(step * 16, 16), 16), chunk * 128:(chunk + 1) * 128] = rows[chunk]
+        for chunk in range(32):
+            start = (half * 32 + chunk) * 128
+            matrix[pl.ds(pl.multiple_of(step * 16, 16), 16), start:start + 128] = rows[chunk]
 
     def ag_y(p, h, d):
         part = gathered.at[p, h, z, k, pl.ds(pl.multiple_of(y * 128, 128), 128)]
@@ -117,19 +118,27 @@
         part = held.at[p + 1, h, frm]
         return copy(part, part, xg_s.at[p, h, d - 1], xg_r.at[p, h, d - 1], row, (x + d) % X)
 
+    def ag_far(p, h, zo, to):
+        part = gathered.at[p, h, zo, k, pl.ds(pl.multiple_of(y * 128, 128), 128)]
+        return copy(part, part, af_s.at[p, h], af_r.at[p, h], at(to, y, k))
+
+    def ag_far_y(p, h, d):
+        part = gathered.at[p, h, z + 4, k, pl.ds(pl.multiple_of(y * 128, 128), 128)]
+        return copy(part, part, ag_s.at[p, h, d - 1], ag_r.at[p, h, d - 1], at(z, (y + d) % Y, k))
+
     def ring_send(way, s):
-        down = (z >= 1) & (z + s - 1 <= 7) & (s <= 4 - k)
+        down = (z >= 1) & (z + s - 1 <= 7) & (s <= 3)
         up_zo = (z + 9 - s) % 8
-        up = (up_zo >= 5 - k) & (s <= 3 + k)
+        up = (up_zo >= 5) & (s <= 3)
         if way == 0:
             return down, z + s - 1, z - 1
         return up, up_zo, (z + 1) % 8
 
-    def ring_get(way, s, kk):
+    def ring_get(way, s):
         if way == 0:
-            return (z + s <= 7) & (s <= 4 - kk), z + s
+            return (z + s <= 7) & (s <= 3), z + s
         zo = (z + 8 - s) % 8
-        return (zo >= 5 - kk) & (s <= 3 + kk), zo
+        return (zo >= 5) & (s <= 3), zo
 
     def columns(zo, kk):
         return pl.ds(pl.multiple_of((zo * C + kk) * 512, 512), 512)
@@ -147,6 +156,10 @@
         gathered[p, h, z, k, pl.ds(pl.multiple_of(y * 128, 128), 128), :] = held[p, h, x]
         for d in range(1, Y):
             ag_y(p, h, d).start()
+
+        @pl.when(z >= 4)
+        def _():
+            ag_far(p, h, z, z - 4).start()
 
     def ag_pass(p, h, s):
         for way in range(2):
@@ -162,6 +175,30 @@
         ag_pass(p, h, 1)
         ag_core(p, h, z, k).start()
 
+    def far_pass(p):
+        @pl.when(z < 4)
+        def _():
+            for h in range(2):
+                ag_far(p, h, z + 4, z).wait_recv()
+                for d in range(1, Y):
+                    ag_far_y(p, h, d).start()
+
+    def far_core(p):
+        @pl.when(z < 4)
+        def _():
+            for h in range(2):
+                for d in range(1, Y):
+                    ag_far_y(p, h, d).wait_recv()
+                ag_core(p, h, z + 4, k).start()
+
+    def far_use(p):
+        @pl.when(z < 4)
+        def _():
+            direct_both(p, z + 4, k)
+            for h in range(2):
+                ag_core(p, h, z + 4, 1 - k).wait_recv()
+            direct_both(p, z + 4, 1 - k)
+
     def ag_own(p):
         acc[...] = jnp.zeros_like(acc)
 
@@ -179,18 +216,18 @@
     def ag_step(p, e):
         s, h = 1 + e // 2, e % 2
         for way in range(2):
-            cond, zo = ring_get(way, s, k)
+            cond, zo = ring_get(way, s)
 
             @pl.when(cond)
             def _():
                 ag_z(p, h, way, s, zo, z).wait_recv()
 
-        @pl.when(s < 4)
+        @pl.when(s < 3)
         def _():
             ag_pass(p, h, s + 1)
 
         for way in range(2):
-            cond, zo = ring_get(way, s, k)
+            cond, zo = ring_get(way, s)
 
             @pl.when(cond & (zo > z))
             def _():
@@ -201,8 +238,8 @@
 
         def use(way, carry):
             kk = k if mine else 1 - k
-            down, zd = ring_get(0, s, kk)
-            up, zu = ring_get(1, s, kk)
+            down, zd = ring_get(0, s)
+            up, zu = ring_get(1, s)
             zo = jnp.where(way == 0, zd, zu)
             cond = ((way == 0) & down | (way == 1) & up) & (zo > z)
 
@@ -211,11 +248,11 @@
                 if not mine:
                     ag_core(p, h, zo, kk).wait_recv()
 
-                @pl.when(s == 4)
+                @pl.when(s == 3)
                 def _():
                     direct_half(p, h, zo, kk)
 
-                @pl.when((s < 4) & (h == 1))
+                @pl.when((s < 3) & (h == 1))
                 def _():
                     direct_both(p, zo, kk)
 
@@ -307,6 +344,16 @@
                 ag_x(p, h, d, (x + X - d) % X).wait_recv()
         out[p] = held[p + 1]
 
+    def build_rest(e):
+        def build_some(part, carry):
+            for n in range(4):
+                build(part * 4 + n, 0)
+            return carry
+
+        @pl.when(z < 4)
+        def _():
+            lax.fori_loop(e * 4, e * 4 + 4, build_some, 0)
+
     def product(p, carry):
         for h in range(2):
             ag_start(p, h)
@@ -316,26 +363,21 @@
             set_up()
 
             def build_some(part, carry):
-                @pl.when(part % (BUILDS // 4) == 0)
+                @pl.when(part % 2 == 0)
                 def _():
-                    load(part // (BUILDS // 4)).wait()
-
-                for n in range(32 // BUILDS):
-                    build(part * (32 // BUILDS) + n)
+                    load(part // 2).wait()
+
+                for n in range(4):
+                    build(part * 4 + n, 1)
 
                 @pl.when(part == FIRST_AFTER)
                 def _():
                     for h in range(2):
                         ag_first(p, h)
 
-                for e, after in enumerate(STEP_AFTER):
-                    @pl.when(part == after)
-                    def _():
-                        ag_step(p, e)
-
                 return carry
 
-            lax.fori_loop(0, BUILDS, build_some, 0)
+            lax.fori_loop(0, 8, build_some, 0)
 
         @pl.when(p == 1)
         def _():
@@ -344,13 +386,14 @@
             collect(0)
 
         make_pt(p)
-        lead = jnp.where(p == 0, -3, 0)
+        lead = jnp.where(p == 0, -2, 0)
+        use = 1 - p
 
         def turn(step, carry):
-            n = step - 6
-
-            def stage(first, body, count=8, skip=0):
-                @pl.when((n >= first + skip) & (n < first + count))
+            n = step - 3
+
+            def stage(first, body, count):
+                @pl.when((n >= first) & (n < first + count))
                 def _():
                     body(n - first)
 
@@ -363,17 +406,21 @@
 
             stage_zo(-3, rs_a)
             stage_zo(-2, rs_b1)
-            stage(lead, lambda e: ag_step(p, e), 8, jnp.where(p == 0, len(STEP_AFTER), 0))
+            stage(lead, lambda e: ag_step(p, e), 6)
+            stage(jnp.where(p == 0, -3, -2), lambda e: far_pass(p), 1)
             stage_zo(0, rs_b2)
             stage_zo(3, rs_c)
-            stage(jnp.where(p == 0, -6, -1), lambda e: ag_own(p), 1)
-            stage(lead, lambda e: ag_use(p, e, True))
-            stage(lead + 1, lambda e: ag_use(p, e, False))
-            stage(lead + 7, lambda e: x_start(p, e), 2)
-            stage(jnp.where(p == 0, 6, 8), lambda e: rs_late(p), 1)
+            stage(jnp.where(p == 0, -1, 1), lambda e: far_core(p), 1)
+            stage(jnp.where(p == 0, -1, 99), build_rest, 2)
+            stage(1 - 2 * p, lambda e: ag_own(p), 1)
+            stage(2, lambda e: far_use(p), 1)
+            stage(use, lambda e: ag_use(p, e, True), 6)
+            stage(use + 1, lambda e: ag_use(p, e, False), 6)
+            stage(use + 5, lambda e: x_start(p, e), 2)
+            stage(jnp.where(p == 0, 6, 7), lambda e: rs_late(p), 1)
             return carry
 
-        lax.fori_loop(0, 17, turn, 0)
+        lax.fori_loop(0, 14, turn, 0)
         rs_d(p)
         for h in range(2):
             finish(p, h)
@@ -381,17 +428,26 @@
 
     pl.semaphore_wait(barrier, 1 + (Y - 1) + (Z - 1) + (X - 1))
     lax.fori_loop(0, 2, product, 0)
-    collect(1)
 
     def left(p, carry):
         for h in range(2):
             for d in range(1, Y):
                 ag_y(p, h, d).wait_send()
+
+            @pl.when(z >= 4)
+            def _():
+                ag_far(p, h, z, z - 4).wait_send()
+
+            @pl.when(z < 4)
+            def _():
+                for d in range(1, Y):
+                    ag_far_y(p, h, d).wait_send()
+
             for d in range(1, X):
                 rs_x(p, h, d).wait_send()
                 ag_x(p, h, d, x).wait_send()
             for way in range(2):
-                for s in range(1, 5):
+                for s in range(1, 4):
                     cond, zo, to = ring_send(way, s)
 
                     @pl.when(cond)
@@ -415,6 +471,7 @@
         return carry
 
     lax.fori_loop(0, 2, left, 0)
+    collect(1)
 
 
 def lay_out(held, out1, out2):
@@ -456,7 +513,9 @@
         pltpu.VMEM((2, 2, X - 1, 128, 128), F32),
         dma((4,)),
         *pair(2, 2, Y - 1),
-        *pair(2, 2, 2, 4),
+        *pair(2, 2, 2, 3),
+        *pair(2, 2),
+        *pair(2, 2, Y - 1),
         *pair(2, 2, Z),
         *pair(2, Z),
         *pair(2, Z, 3),

time: 104 us -> 98.2 us (0.944)
  Pallas kernels: 103 us -> 97.5 us
    pallas_call x1, Pallas kernels: 101 us -> 95.5 us  [per_device(): pl.pallas_call(kernel, out_shape=jax.ShapeDtypeStruct((2, 2, X, 128, 128)...]
where the time goes in v3:
time: 98.2 us; the launch traced here: 98.1 us
  Pallas kernels  97.5 us (99%)
    pallas_call x1, Pallas kernels, per_device(): pl.pallas_call(kernel, out_shape=jax.ShapeDtypeStruct((2, 2, X, 128, 128)...  95.5 us

profile of v3, /device:TPU:192, one launch (start us, length us, event | category | flops | bytes accessed | tf_op | source)
XLA Modules:
  0.0 98.1 jit_solution(16445061377841839623)
XLA Ops:
  0.6 95.5 %shard_map.59.held = bf16[2,2,4,128,128]{4,3,2,1,0:T(8,128)(2,1)} custom-call(bf16[512,256]{1,0:T(8,128)(2,1)} %panel.1, bf16[384,4096]{1,0:T(8,128)(2,1)} %blocks.1, s32[384]{0:T(512)} %block_row.1, s32[384]{0:T(512)} %block_slot.1), custom_call_target="tpu_custom_call" | custom-call | tf_op jit(solution)/shard_map/pallas_call | solution.py:526
  96.2 1.9 %shard_map.60 = (bf16[512,256]{1,0:T(8,128)(2,1)}, bf16[512,256]{1,0:T(8,128)(2,1)}) custom-call(bf16[2,2,4,128,128]{4,3,2,1,0:T(8,128)(2,1)} %shard_map.59.held), custom_call_target="tpu_custom_call" | custom-call | tf_op jit(solution)/shard_map/pallas_call | solution.py:536

commit v4 on v3

--- a/solution.py
+++ b/solution.py
@@ -405,10 +405,10 @@
                     body(p, zo)
 
             stage_zo(-3, rs_a)
-            stage_zo(-2, rs_b1)
+            stage_zo(-1, rs_b1)
             stage(lead, lambda e: ag_step(p, e), 6)
             stage(jnp.where(p == 0, -3, -2), lambda e: far_pass(p), 1)
-            stage_zo(0, rs_b2)
+            stage_zo(1, rs_b2)
             stage_zo(3, rs_c)
             stage(jnp.where(p == 0, -1, 1), lambda e: far_core(p), 1)
             stage(jnp.where(p == 0, -1, 99), build_rest, 2)

time: 98.2 us -> 97.2 us (0.990)
  Pallas kernels: 97.5 us -> 96.4 us
    pallas_call x1, Pallas kernels: 95.5 us -> 94.5 us  [per_device(): pl.pallas_call(kernel, out_shape=jax.ShapeDtypeStruct((2, 2, X, 128, 128)...]
where the time goes in v4:
time: 97.2 us; the launch traced here: 97.1 us
  Pallas kernels  96.4 us (99%)
    pallas_call x1, Pallas kernels, per_device(): pl.pallas_call(kernel, out_shape=jax.ShapeDtypeStruct((2, 2, X, 128, 128)...  94.5 us

profile of v4, /device:TPU:192, one launch (start us, length us, event | category | flops | bytes accessed | tf_op | source)
XLA Modules:
  0.0 97.1 jit_solution(7374266931884878233)
XLA Ops:
  0.6 94.5 %shard_map.59.held = bf16[2,2,4,128,128]{4,3,2,1,0:T(8,128)(2,1)} custom-call(bf16[512,256]{1,0:T(8,128)(2,1)} %panel.1, bf16[384,4096]{1,0:T(8,128)(2,1)} %blocks.1, s32[384]{0:T(512)} %block_row.1, s32[384]{0:T(512)} %block_slot.1), custom_call_target="tpu_custom_call" | custom-call | tf_op jit(solution)/shard_map/pallas_call | solution.py:526
  95.1 1.9 %shard_map.60 = (bf16[512,256]{1,0:T(8,128)(2,1)}, bf16[512,256]{1,0:T(8,128)(2,1)}) custom-call(bf16[2,2,4,128,128]{4,3,2,1,0:T(8,128)(2,1)} %shard_map.59.held), custom_call_target="tpu_custom_call" | custom-call | tf_op jit(solution)/shard_map/pallas_call | solution.py:536

commit v5 on v4

--- a/solution.py
+++ b/solution.py
@@ -411,13 +411,13 @@
             stage_zo(1, rs_b2)
             stage_zo(3, rs_c)
             stage(jnp.where(p == 0, -1, 1), lambda e: far_core(p), 1)
-            stage(jnp.where(p == 0, -1, 99), build_rest, 2)
+            stage(jnp.where(p == 0, -2, 99), build_rest, 2)
             stage(1 - 2 * p, lambda e: ag_own(p), 1)
             stage(2, lambda e: far_use(p), 1)
             stage(use, lambda e: ag_use(p, e, True), 6)
             stage(use + 1, lambda e: ag_use(p, e, False), 6)
             stage(use + 5, lambda e: x_start(p, e), 2)
-            stage(jnp.where(p == 0, 6, 7), lambda e: rs_late(p), 1)
+            stage(jnp.where(p == 0, 5, 6), lambda e: rs_late(p), 1)
             return carry
 
         lax.fori_loop(0, 14, turn, 0)

time: 97.2 us -> 94.8 us (0.975); the launches traced: 97.1 us -> 93.6 us
  Pallas kernels: 96.4 us -> 93 us
    pallas_call x1, Pallas kernels: 94.5 us -> 91 us  [per_device(): pl.pallas_call(kernel, out_shape=jax.ShapeDtypeStruct((2, 2, X, 128, 128)...]
where the time goes in v5:
time: 94.8 us; the launch traced here: 93.6 us
  Pallas kernels  93 us (98%)
    pallas_call x1, Pallas kernels, per_device(): pl.pallas_call(kernel, out_shape=jax.ShapeDtypeStruct((2, 2, X, 128, 128)...  91 us
    pallas_call x1, Pallas kernels, per_device(): pl.pallas_call(lay_out, out_shape=(shape, shape), in_specs=[vmem], out_sp...  1.92 us

profile of v5, /device:TPU:192, one launch (start us, length us, event | category | flops | bytes accessed | tf_op | source)
XLA Modules:
  0.0 93.6 jit_solution(8606949160502831729)
XLA Ops:
  0.6 91.0 %shard_map.59.held = bf16[2,2,4,128,128]{4,3,2,1,0:T(8,128)(2,1)} custom-call(bf16[512,256]{1,0:T(8,128)(2,1)} %panel.1, bf16[384,4096]{1,0:T(8,128)(2,1)} %blocks.1, s32[384]{0:T(512)} %block_row.1, s32[384]{0:T(512)} %block_slot.1), custom_call_target="tpu_custom_call" | custom-call | tf_op jit(solution)/shard_map/pallas_call | solution.py:526
  91.7 1.9 %shard_map.60 = (bf16[512,256]{1,0:T(8,128)(2,1)}, bf16[512,256]{1,0:T(8,128)(2,1)}) custom-call(bf16[2,2,4,128,128]{4,3,2,1,0:T(8,128)(2,1)} %shard_map.59.held), custom_call_target="tpu_custom_call" | custom-call | tf_op jit(solution)/shard_map/pallas_call | solution.py:536
